TPU v7x, 32 devices: a whole 2x2x4 slice. The times are simulated.
32 devices in a mesh: band: 4 (over x, core), span: 8 (over z, y).
Axes of the slice: x: 2, y: 2, z: 4, core: 2. Of those that a mesh axis runs over, the one named last changes fastest.
Arguments:
- gases: bfloat16 [7, 32, 16384], P(None, None, ('band', 'span')), may hold values from 0 to 1
- pressure_bin: int32 [32, 16384], P(None, ('band', 'span')), may hold values from 0 to 59
- layer_mass: bfloat16 [32, 16384], P(None, ('band', 'span')), may hold values from 0.5 to 2
- cos_zenith: bfloat16 [16384], P(('band', 'span')), may hold values from 0.19921875 to 1
- surface_albedo: bfloat16 [16384], P(('band', 'span')), may hold values from 0.049804688 to 0.8984375
- column_order: int32 [16384], P(('band', 'span')), may hold values from 0 to 511, as said below
- sunlit: int32 [128], P(('band', 'span')), may hold values from 0 to 1, as said below
- absorption: bfloat16 [112, 7, 60], replicated, may hold values from 9.9658966e-05 to 0.099609375
- scattering: bfloat16 [112, 60], replicated, may hold values from 0.19921875 to 0.94921875
Outputs:
- heating: float32 [32, 16384], P(None, ('band', 'span'))
Inputs may be any that keep to these rules, and one draw needn't show every extreme that they name: `column_order`: the 512 entries of each device's slice are a permutation of 0 to 511. The 4 devices with the same index along the second mesh axis hold 8 sunlit blocks together; among them one device has all 4 blocks sunlit and one has none.
All inputs are finite; a program needn't handle non-finite values.
Results may differ from a plain program's by a relative error of at most 0.0003.
Values may be sent and summed in bfloat16 or wider, within the bound.
No kernel may reach another device: no remote copies, remote signals or barrier semaphores. Data moves between devices by JAX's collectives and lax.ppermute only.
A program may use at most 64 MiB of HBM per device.

v0:
```python
import functools
import math

import jax
import jax.numpy as jnp
from jax import lax
from jax.experimental import pallas as pl
from jax.experimental.pallas import tpu as pltpu
from jax.sharding import PartitionSpec as P

LANES = 128
ROWS = 8
PACK = 16
STEP = 8
HALVES = 2
BIN_ROWS = 64
LOG2E = math.log2(math.e)
VMEM_BYTES = 24 * 1024 * 1024


def one_hot(hit):
    return jnp.where(hit, 1.0, 0.0).astype(jnp.bfloat16)


def prepare_kernel(
    per_peer,
    sunlit_hbm,
    gases_hbm,
    bins_hbm,
    cosine_hbm,
    ground_hbm,
    order_hbm,
    absorb_hbm,
    scatter_hbm,
    wanted_hbm,
    table_ref,
    scatter_ref,
    block_ref,
    owner_ref,
    sunlit_ref,
    gases_ref,
    bins_ref,
    cosine_ref,
    ground_ref,
    order_ref,
    absorb_ref,
    albedo_ref,
    wanted_ref,
    copied,
    wide_buf,
):
    gas_count, levels, columns = gases_ref.shape
    points = table_ref.shape[0]
    bin_count = absorb_ref.shape[1]
    blocks = columns // LANES
    bin_row = gas_count * levels
    ray_row = bin_row + levels
    first_row = gas_count * BIN_ROWS
    peers = wanted_ref.shape[0]

    copies = [
        pltpu.make_async_copy(source, target, copied.at[place])
        for place, (source, target) in enumerate(
            (
                (sunlit_hbm, sunlit_ref),
                (order_hbm, order_ref),
                (absorb_hbm, absorb_ref),
                (scatter_hbm, albedo_ref),
                (cosine_hbm, cosine_ref),
                (ground_hbm, ground_ref),
                (bins_hbm, bins_ref),
                (gases_hbm, gases_ref),
            )
        )
    ]
    for copy in copies:
        copy.start()
    wide_buf[...] = jnp.zeros_like(wide_buf)
    copies[0].wait()
    for peer in range(peers):
        wanted_ref[peer] = jnp.full((1, 1), sunlit_ref[peer * sunlit_ref.shape[0] // peers], jnp.int32)
    sending = pltpu.make_async_copy(wanted_ref, wanted_hbm, copied.at[len(copies)])
    sending.start()
    for copy in copies[1:4]:
        copy.wait()

    square = (columns, columns)
    order = jnp.broadcast_to(order_ref[...], square)
    match = one_hot(order == lax.broadcasted_iota(jnp.int32, square, 0))
    place = lax.broadcasted_iota(jnp.int32, (ROWS, columns), 1)
    group = (place // per_peer).astype(jnp.float32).astype(jnp.bfloat16)
    owner_ref[...] = lax.dot_general(group, match, (((1,), (1,)), ((), ())), preferred_element_type=jnp.float32)

    for gas in range(gas_count):
        wide_buf[gas * BIN_ROWS : gas * BIN_ROWS + bin_count, :points] = absorb_ref[gas].astype(jnp.float32)
    wide_buf[first_row : first_row + bin_count, :points] = 0.5 * albedo_ref[...].astype(jnp.float32)
    turned = [
        jnp.transpose(wide_buf[i * LANES : (i + 1) * LANES])[:points].astype(jnp.bfloat16)
        for i in range(wide_buf.shape[0] // LANES)
    ]
    whole = jnp.concatenate(turned, axis=1)
    table_ref[...] = whole[:, :first_row]
    scatter_ref[...] = whole[:, first_row : first_row + BIN_ROWS]
    for copy in copies[4:]:
        copy.wait()

    for block in range(blocks):
        cols = slice(block * LANES, (block + 1) * LANES)
        for gas in range(gas_count):
            block_ref[block, gas * levels : (gas + 1) * levels] = gases_ref[gas, :, cols].astype(jnp.float32)
        block_ref[block, bin_row:ray_row] = bins_ref[:, cols].astype(jnp.float32)
    wide = (1, columns)
    cosines = cosine_ref[...].astype(jnp.float32).reshape(wide)
    grounds = ground_ref[...].astype(jnp.float32).reshape(wide)
    for block in range(blocks):
        cols = slice(block * LANES, (block + 1) * LANES)
        block_ref[block, ray_row : ray_row + ROWS] = jnp.broadcast_to(cosines[:, cols], (ROWS, LANES))
        block_ref[block, ray_row + ROWS : ray_row + 2 * ROWS] = jnp.broadcast_to(grounds[:, cols], (ROWS, LANES))
    sending.wait()


def heating_kernel(
    mass_hbm,
    table_ref,
    scatter_ref,
    block_ref,
    heat_ref,
    mass_ref,
    copied,
    optic_ref,
    up_buf,
    rise_buf,
    pass_buf,
    refl_buf,
    fall_buf,
    direct_buf,
    gain_buf,
    net_buf,
    warm_ref,
):
    levels, columns = heat_ref.shape
    points, gas_rows = table_ref.shape
    gas_count = gas_rows // BIN_ROWS
    half = points // HALVES
    vregs = half // ROWS
    blocks = columns // LANES
    bin_row = gas_count * levels
    ray_row = bin_row + levels
    mass_copy = pltpu.make_async_copy(mass_hbm, mass_ref, copied)
    mass_copy.start()

    def optical(slot, layer):
        parts = []
        shape = (BIN_ROWS, LANES)
        rows = lax.broadcasted_iota(jnp.int32, shape, 0).astype(jnp.float32).astype(jnp.bfloat16)
        one = jnp.ones(shape, jnp.bfloat16)
        zero = jnp.zeros(shape, jnp.bfloat16)
        selectors = []
        for near in (layer, layer + 1):
            place = bin_row + near
            bins = jnp.broadcast_to(block_ref[slot, place : place + 1, :], (PACK, LANES)).astype(jnp.bfloat16)
            bins = jnp.concatenate([bins] * (BIN_ROWS // PACK), axis=0)
            selectors.append(jnp.where(bins == rows, one, zero))
        for gas in range(gas_count):
            pair = []
            for near, selector in zip((layer, layer + 1), selectors):
                place = gas * levels + near
                amount = jnp.broadcast_to(block_ref[slot, place : place + 1, :], (PACK, LANES)).astype(jnp.bfloat16)
                pair.append(jnp.concatenate([amount] * (BIN_ROWS // PACK), axis=0) * selector)
            parts.append(jnp.concatenate(pair, axis=1))
        weighted = jnp.concatenate(parts, axis=0)
        selected = jnp.concatenate(selectors, axis=1)
        tau = jnp.dot(table_ref[...], weighted, preferred_element_type=jnp.float32)
        albedo = jnp.dot(scatter_ref[...], selected, preferred_element_type=jnp.float32)
        for near in range(2):
            cols = slice(near * LANES, (near + 1) * LANES)
            optic_ref[layer + near, :points] = tau[:, cols]
            optic_ref[layer + near, points:] = albedo[:, cols]

    def advance(first, part, cosine, slope):
        rows = slice(part * half, (part + 1) * half)
        half_rows = slice(points + part * half, points + (part + 1) * half)
        shape = (vregs, ROWS, LANES)
        if first > 0:
            refl = refl_buf[rows].reshape(shape)
            fall = fall_buf[rows].reshape(shape)
            direct = direct_buf[rows].reshape(shape)
        else:
            direct = jnp.broadcast_to(cosine[None], shape)
        for layer in range(first, first + STEP):
            tau = optic_ref[layer, rows].reshape(shape)
            half_albedo = optic_ref[layer, half_rows].reshape(shape)
            fading = jnp.exp2(tau * (-1.66 * LOG2E))
            passed = jnp.exp2(tau * slope)
            reflect = half_albedo * (1.0 - fading)
            transmit = fading + reflect
            below = direct * passed
            source = half_albedo * (direct - below)
            if layer == 0:
                up_buf[layer, rows] = transmit.reshape(half, LANES)
                rise_buf[layer, rows] = source.reshape(half, LANES)
                fall = source
                refl = reflect
            else:
                pass_buf[layer, rows] = (1.0 - refl).reshape(half, LANES)
                inverse = pl.reciprocal(1.0 - reflect * refl, approx=True)
                up = transmit * inverse
                rise = (reflect * fall + source) * inverse
                up_buf[layer, rows] = up.reshape(half, LANES)
                rise_buf[layer, rows] = rise.reshape(half, LANES)
                fall = source + transmit * (fall + refl * rise)
                refl = reflect + transmit * (refl * up)
            direct = below
            gain_buf[part, layer + 1] = jnp.sum(direct + fall, axis=0)
        refl_buf[rows] = refl.reshape(half, LANES)
        fall_buf[rows] = fall.reshape(half, LANES)
        direct_buf[rows] = direct.reshape(half, LANES)

    lead = range(0, STEP, 2)

    def column_block(block, carry):
        cosine = block_ref[block, ray_row : ray_row + ROWS]
        slope = (-LOG2E) / cosine
        for part in range(HALVES):
            gain_buf[part, 0] = cosine * float(vregs)
        for first in range(0, levels, STEP):
            coming = [layer for layer in range(first + STEP, first + 2 * STEP, 2) if layer < levels]
            for part in range(HALVES):
                for layer in coming[part * len(coming) // HALVES : (part + 1) * len(coming) // HALVES]:
                    optical(block, layer)
                advance(first, part, cosine, slope)

        following = jnp.minimum(block + 1, blocks - 1)
        for layer in lead:
            optical(following, layer)

        albedo = block_ref[block, ray_row + ROWS : ray_row + 2 * ROWS]
        shape = (points // ROWS, ROWS, LANES)
        refl = refl_buf[...].reshape(shape)
        arriving = (fall_buf[...] + direct_buf[...]).reshape(shape)
        rising = albedo * arriving * pl.reciprocal(1.0 - albedo * refl, approx=True)

        def total(level):
            summed = gain_buf[0, level]
            for part in range(1, HALVES):
                summed = summed + gain_buf[part, level]
            return summed

        net_buf[levels] = total(levels) - jnp.sum(rising * (1.0 - refl), axis=0)
        for layer in range(levels - 1, -1, -1):
            rising = up_buf[layer].reshape(shape) * rising + rise_buf[layer].reshape(shape)
            taken = rising if layer == 0 else rising * pass_buf[layer].reshape(shape)
            net_buf[layer] = total(layer) - jnp.sum(taken, axis=0)
        warm_ref[block] = jnp.sum(net_buf[:levels] - net_buf[1:], axis=1)
        return carry

    for layer in lead:
        optical(0, layer)
    lax.fori_loop(0, blocks, column_block, 0)
    mass_copy.wait()

    for block in range(blocks):
        cols = slice(block * LANES, (block + 1) * LANES)
        heat_ref[:, cols] = warm_ref[block] / mass_ref[:, cols].astype(jnp.float32)


def shade_kernel(heat_ref, owner_ref, flags_ref, out_ref):
    owner = owner_ref[...]
    lit = jnp.zeros_like(owner)
    for group in range(flags_ref.shape[0]):
        flag = jnp.broadcast_to(flags_ref[group].astype(jnp.float32), owner.shape)
        lit = jnp.where(owner == float(group), flag, lit)
    out_ref[...] = heat_ref[...] * lit[:1]


def local(
    gases,
    pressure_bin,
    layer_mass,
    cos_zenith,
    surface_albedo,
    column_order,
    sunlit,
    absorption,
    scattering,
):
    group_size = lax.axis_size("span")
    gas_count, levels, columns = gases.shape
    points, _, bins = absorption.shape
    rows = gas_count * levels + levels + PACK
    blocks = columns // LANES
    gas_rows = gas_count * BIN_ROWS
    hbm = pl.BlockSpec(memory_space=pltpu.HBM)
    vmem = pl.BlockSpec(memory_space=pltpu.VMEM)

    def pinned(*operands):
        return [pltpu.with_memory_space_constraint(operand, pltpu.HBM) for operand in operands]

    params = pltpu.CompilerParams(vmem_limit_bytes=VMEM_BYTES)
    wanted, table, scatter, block, owner = pl.pallas_call(
        functools.partial(prepare_kernel, columns // group_size),
        out_shape=(
            jax.ShapeDtypeStruct((group_size, 1, 1), sunlit.dtype),
            jax.ShapeDtypeStruct((points, gas_rows), jnp.bfloat16),
            jax.ShapeDtypeStruct((points, BIN_ROWS), jnp.bfloat16),
            jax.ShapeDtypeStruct((blocks, rows, LANES), jnp.float32),
            jax.ShapeDtypeStruct((ROWS, columns), jnp.float32),
        ),
        in_specs=[hbm] * 8,
        out_specs=(hbm, vmem, vmem, vmem, vmem),
        scratch_shapes=[
            pltpu.SMEM(sunlit.shape, sunlit.dtype),
            pltpu.VMEM(gases.shape, gases.dtype),
            pltpu.VMEM(pressure_bin.shape, pressure_bin.dtype),
            pltpu.VMEM(cos_zenith.shape, cos_zenith.dtype),
            pltpu.VMEM(surface_albedo.shape, surface_albedo.dtype),
            pltpu.VMEM((1, columns), column_order.dtype),
            pltpu.VMEM((gas_count, bins, points), absorption.dtype),
            pltpu.VMEM((bins, points), scattering.dtype),
            pltpu.VMEM((group_size, 1, 1), sunlit.dtype),
            pltpu.SemaphoreType.DMA((9,)),
            pltpu.VMEM((-(-(gas_rows + BIN_ROWS) // LANES) * LANES, LANES), jnp.float32),
        ],
        compiler_params=params,
    )(
        *pinned(
            sunlit,
            gases,
            pressure_bin,
            cos_zenith,
            surface_albedo,
            column_order.reshape(1, columns),
            jnp.transpose(absorption, (1, 2, 0)),
            jnp.transpose(scattering),
        )
    )
    flags = lax.all_to_all(wanted, "span", split_axis=0, concat_axis=0, tiled=True)
    field = pltpu.VMEM((levels, points, LANES), jnp.float32)
    state = pltpu.VMEM((points, LANES), jnp.float32)
    heat = pl.pallas_call(
        heating_kernel,
        out_shape=jax.ShapeDtypeStruct((levels, columns), jnp.float32),
        in_specs=[hbm, vmem, vmem, vmem],
        out_specs=vmem,
        scratch_shapes=[
            pltpu.VMEM(layer_mass.shape, layer_mass.dtype),
            pltpu.SemaphoreType.DMA(()),
            pltpu.VMEM((levels, 2 * points, LANES), jnp.float32),
            field,
            field,
            field,
            state,
            state,
            state,
            pltpu.VMEM((HALVES, levels + 1, ROWS, LANES), jnp.float32),
            pltpu.VMEM((levels + 1, ROWS, LANES), jnp.float32),
            pltpu.VMEM((blocks, levels, LANES), jnp.float32),
        ],
        compiler_params=params,
        cost_estimate=pl.CostEstimate(
            flops=40 * levels * points * columns, bytes_accessed=1 << 20, transcendentals=3 * levels * points * columns
        ),
    )(*pinned(layer_mass), table, scatter, block)
    return pl.pallas_call(
        shade_kernel,
        out_shape=jax.ShapeDtypeStruct((levels, columns), heat.dtype),
        in_specs=[vmem] * 3,
        out_specs=vmem,
        compiler_params=params,
    )(heat, owner, flags)


def solution(mesh):
    placed = (
        P(None, None, ("band", "span")),
        P(None, ("band", "span")),
        P(None, ("band", "span")),
        P(("band", "span")),
        P(("band", "span")),
        P(("band", "span")),
        P(("band", "span")),
        P(),
        P(),
    )
    return jax.shard_map(
        local, mesh=mesh, in_specs=placed, out_specs=P(None, ("band", "span")), check_vma=False
    )
```

profile of v0, /device:TPU:0, one launch (start us, length us, event | category | flops | bytes accessed | tf_op | source)
XLA Modules:
  0.0 19.8 jit_solution(10652876998256677947)
XLA Ops:
  0.0 1.4 %shard_map.91 = (s32[8,1,1]{2,1,0:T(1,128)}, bf16[112,448]{1,0:T(8,128)(2,1)S(1)}, bf16[112,64]{1,0:T(8,128)(2,1)S(1)}, f32[4,272,128]{2,1,0:T(8,128)S(1)}, f32[8,512]{1,0:T(8,128)S(1)}) custom-call(s32[4]{0:T(128)} %sunlit_hbm.1, bf16[7,32,512]{2,1,0:T(8,128)(2,1)} %gases_hbm.1, s32[32,512]{1,0:T(8,128)} %bins_hbm.1, bf16[512]{0:T(512)(128)(2,1)} %cosine_hbm.1, ...), custom_call_target="tpu_custom_call" | custom-call | tf_op jit(solution)/shard_map/pallas_call | solution.py:300
  1.4 7.3 %all-to-all-start = ((s32[8,1,1]{2,1,0:T(1,128)}), s32[8,1,1]{2,1,0:T(1,128)S(1)}, u32[]{:S(2)}, u32[]{:S(2)}) async-start(s32[8,1,1]{2,1,0:T(1,128)} %get-tuple-element.14), calls=%async_computation | async-start | bytes 8192 | tf_op jit(solution)/shard_map/all_to_all | solution.py:337
  8.7 10.4 %shard_map.92.heat_ref = f32[32,512]{1,0:T(8,128)S(1)} custom-call(bf16[32,512]{1,0:T(8,128)(2,1)} %mass_hbm.1, bf16[112,448]{1,0:T(8,128)(2,1)S(1)} %get-tuple-element.10.table_ref, bf16[112,64]{1,0:T(8,128)(2,1)S(1)} %get-tuple-element.11.scatter_ref, f32[4,272,128]{2,1,0:T(8,128)S(1)} %get-tuple-element.12.block_ref), custom_call_target="tpu_custom_call" | custom-call | flops 73400320 | bytes 1048576 | tf_op jit(solution)/shard_map/pallas_call | solution.py:340
  19.1 0.0 all-to-all-done.flags_ref
  19.1 0.7 %shard_map.93 = f32[32,512]{1,0:T(8,128)} custom-call(f32[32,512]{1,0:T(8,128)S(1)} %shard_map.92.heat_ref, f32[8,512]{1,0:T(8,128)S(1)} %get-tuple-element.13.owner_ref, s32[8,1,1]{2,1,0:T(1,128)S(1)} %all-to-all-done.flags_ref), custom_call_target="tpu_custom_call" | custom-call | tf_op jit(solution)/shard_map/pallas_call | solution.py:364
Async XLA Ops:
  1.4 17.7 %all-to-all-start = ((s32[8,1,1]{2,1,0:T(1,128)}), s32[8,1,1]{2,1,0:T(1,128)S(1)}, u32[]{:S(2)}, u32[]{:S(2)}) async-start(s32[8,1,1]{2,1,0:T(1,128)} %get-tuple-element.14), calls=%async_computation | async-start | bytes 8192 | tf_op jit(solution)/shard_map/all_to_all | solution.py:337
where the time goes:
time: 20 us; the launch traced here: 19.8 us
  Pallas kernels  12.5 us (62%)
  starting transfers between devices  7.29 us (36%)
    pallas_call x1, Pallas kernels, local(): pl.pallas_call(heating_kernel, out_shape=jax.ShapeDtypeStruct((levels, co...  10.4 us
    all_to_all x1, starting transfers between devices, local(): lax.all_to_all(wanted, 'span', split_axis=0, concat_axis=0, tiled=True)  7.29 us
    pallas_call x1, Pallas kernels, local(): pl.pallas_call(functools.partial(prepare_kernel, columns // group_size),...  1.37 us
    pallas_call x1, Pallas kernels, local(): pl.pallas_call(shade_kernel, out_shape=jax.ShapeDtypeStruct((levels, colu...  0.71 us
  transfers between devices with their start and end apart: 1, of which 0 were waited for; matrix products, arithmetic and copies ran while one was open for 0% of the time, Pallas kernels for 53%

commit v1 on v0

--- a/solution.py
+++ b/solution.py
@@ -15,7 +15,7 @@
 HALVES = 2
 BIN_ROWS = 64
 LOG2E = math.log2(math.e)
-VMEM_BYTES = 24 * 1024 * 1024
+VMEM_BYTES = 32 * 1024 * 1024
 
 
 def one_hot(hit):
@@ -128,13 +128,19 @@
     mass_ref,
     copied,
     optic_ref,
-    up_buf,
-    rise_buf,
-    pass_buf,
+    even_up,
+    even_rise,
+    even_pass,
+    even_start,
+    even_gain,
+    odd_up,
+    odd_rise,
+    odd_pass,
+    odd_start,
+    odd_gain,
     refl_buf,
     fall_buf,
     direct_buf,
-    gain_buf,
     net_buf,
     warm_ref,
 ):
@@ -177,7 +183,8 @@
             optic_ref[layer + near, :points] = tau[:, cols]
             optic_ref[layer + near, points:] = albedo[:, cols]
 
-    def advance(first, part, cosine, slope):
+    def advance(first, part, cosine, slope, kept):
+        up_buf, rise_buf, pass_buf, _, gain_buf = kept
         rows = slice(part * half, (part + 1) * half)
         half_rows = slice(points + part * half, points + (part + 1) * half)
         shape = (vregs, ROWS, LANES)
@@ -217,46 +224,70 @@
         direct_buf[rows] = direct.reshape(half, LANES)
 
     lead = range(0, STEP, 2)
-
-    def column_block(block, carry):
+    whole = (points // ROWS, ROWS, LANES)
+
+    def total(gain_buf, level):
+        summed = gain_buf[0, level]
+        for part in range(1, HALVES):
+            summed = summed + gain_buf[part, level]
+        return summed
+
+    def descend(block, kept, other):
         cosine = block_ref[block, ray_row : ray_row + ROWS]
         slope = (-LOG2E) / cosine
+        gain_buf = kept[4]
         for part in range(HALVES):
             gain_buf[part, 0] = cosine * float(vregs)
+        rising = other[3][...].reshape(whole)
+        following = jnp.minimum(block + 1, blocks - 1)
         for first in range(0, levels, STEP):
-            coming = [layer for layer in range(first + STEP, first + 2 * STEP, 2) if layer < levels]
+            coming = [(block, layer) for layer in range(first + STEP, first + 2 * STEP, 2) if layer < levels]
+            if not coming:
+                coming = [(following, layer) for layer in lead]
             for part in range(HALVES):
-                for layer in coming[part * len(coming) // HALVES : (part + 1) * len(coming) // HALVES]:
-                    optical(block, layer)
-                advance(first, part, cosine, slope)
-
-        following = jnp.minimum(block + 1, blocks - 1)
-        for layer in lead:
-            optical(following, layer)
-
+                for where, layer in coming[part * len(coming) // HALVES : (part + 1) * len(coming) // HALVES]:
+                    optical(where, layer)
+                advance(first, part, cosine, slope, kept)
+                if part == 0:
+                    rising = ascend(levels - first, rising, other)
         albedo = block_ref[block, ray_row + ROWS : ray_row + 2 * ROWS]
-        shape = (points // ROWS, ROWS, LANES)
-        refl = refl_buf[...].reshape(shape)
-        arriving = (fall_buf[...] + direct_buf[...]).reshape(shape)
-        rising = albedo * arriving * pl.reciprocal(1.0 - albedo * refl, approx=True)
-
-        def total(level):
-            summed = gain_buf[0, level]
-            for part in range(1, HALVES):
-                summed = summed + gain_buf[part, level]
-            return summed
-
-        net_buf[levels] = total(levels) - jnp.sum(rising * (1.0 - refl), axis=0)
-        for layer in range(levels - 1, -1, -1):
-            rising = up_buf[layer].reshape(shape) * rising + rise_buf[layer].reshape(shape)
-            taken = rising if layer == 0 else rising * pass_buf[layer].reshape(shape)
-            net_buf[layer] = total(layer) - jnp.sum(taken, axis=0)
+        refl = refl_buf[...].reshape(whole)
+        arriving = (fall_buf[...] + direct_buf[...]).reshape(whole)
+        started = albedo * arriving * pl.reciprocal(1.0 - albedo * refl, approx=True)
+        kept[3][...] = started.reshape(points, LANES)
+        gain_buf[0, levels] = gain_buf[0, levels] - jnp.sum(started * (1.0 - refl), axis=0)
+
+    def ascend(end, rising, kept):
+        up_buf, rise_buf, pass_buf, _, gain_buf = kept
+        if end == levels:
+            net_buf[levels] = total(gain_buf, levels)
+        for layer in range(end - 1, end - STEP - 1, -1):
+            rising = up_buf[layer].reshape(whole) * rising + rise_buf[layer].reshape(whole)
+            taken = rising if layer == 0 else rising * pass_buf[layer].reshape(whole)
+            net_buf[layer] = total(gain_buf, layer) - jnp.sum(taken, axis=0)
+        return rising
+
+    def finish(block):
         warm_ref[block] = jnp.sum(net_buf[:levels] - net_buf[1:], axis=1)
+
+    even = (even_up, even_rise, even_pass, even_start, even_gain)
+    odd = (odd_up, odd_rise, odd_pass, odd_start, odd_gain)
+
+    def block_pair(pair, carry):
+        block = 2 * pair
+        descend(block, even, odd)
+        finish(jnp.where(pair == 0, blocks, block - 1))
+        descend(block + 1, odd, even)
+        finish(block)
         return carry
 
     for layer in lead:
         optical(0, layer)
-    lax.fori_loop(0, blocks, column_block, 0)
+    lax.fori_loop(0, blocks // 2, block_pair, 0)
+    rising = odd_start[...].reshape(whole)
+    for first in range(0, levels, STEP):
+        rising = ascend(levels - first, rising, odd)
+    finish(blocks - 1)
     mass_copy.wait()
 
     for block in range(blocks):
@@ -337,6 +368,7 @@
     flags = lax.all_to_all(wanted, "span", split_axis=0, concat_axis=0, tiled=True)
     field = pltpu.VMEM((levels, points, LANES), jnp.float32)
     state = pltpu.VMEM((points, LANES), jnp.float32)
+    kept = (field, field, field, state, pltpu.VMEM((HALVES, levels + 1, ROWS, LANES), jnp.float32))
     heat = pl.pallas_call(
         heating_kernel,
         out_shape=jax.ShapeDtypeStruct((levels, columns), jnp.float32),
@@ -346,15 +378,13 @@
             pltpu.VMEM(layer_mass.shape, layer_mass.dtype),
             pltpu.SemaphoreType.DMA(()),
             pltpu.VMEM((levels, 2 * points, LANES), jnp.float32),
-            field,
-            field,
-            field,
+            *kept,
+            *kept,
             state,
             state,
             state,
-            pltpu.VMEM((HALVES, levels + 1, ROWS, LANES), jnp.float32),
             pltpu.VMEM((levels + 1, ROWS, LANES), jnp.float32),
-            pltpu.VMEM((blocks, levels, LANES), jnp.float32),
+            pltpu.VMEM((blocks + 1, levels, LANES), jnp.float32),
         ],
         compiler_params=params,
         cost_estimate=pl.CostEstimate(

time: 20 us -> 20.6 us (1.030)
  Pallas kernels: 12.5 us -> 13.1 us
    pallas_call x1, Pallas kernels: 10.4 us -> 11 us  [local(): pl.pallas_call(heating_kernel, out_shape=jax.ShapeDtypeStruct((levels, co...]
  transfers between devices with their start and end apart: 1 -> 1, of which waited for: 0 -> 0; matrix products, arithmetic and copies ran while one was open for 0% -> 0% of each run, Pallas kernels for 53% -> 54%
where the time goes in v1:
time: 20.6 us; the launch traced here: 20.4 us
  Pallas kernels  13.1 us (64%)
  starting transfers between devices  7.29 us (35%)
    pallas_call x1, Pallas kernels, local(): pl.pallas_call(heating_kernel, out_shape=jax.ShapeDtypeStruct((levels, co...  11 us
    all_to_all x1, starting transfers between devices, local(): lax.all_to_all(wanted, 'span', split_axis=0, concat_axis=0, tiled=True)  7.29 us
    pallas_call x1, Pallas kernels, local(): pl.pallas_call(functools.partial(prepare_kernel, columns // group_size),...  1.37 us
    pallas_call x1, Pallas kernels, local(): pl.pallas_call(shade_kernel, out_shape=jax.ShapeDtypeStruct((levels, colu...  0.71 us
  transfers between devices with their start and end apart: 1, of which 0 were waited for; matrix products, arithmetic and copies ran while one was open for 0% of the time, Pallas kernels for 54%

profile of v1, /device:TPU:0, one launch (start us, length us, event | category | flops | bytes accessed | tf_op | source)
XLA Modules:
  0.0 20.4 jit_solution(2733504571118394929)
XLA Ops:
  0.0 1.4 %shard_map.91 = (s32[8,1,1]{2,1,0:T(1,128)}, bf16[112,448]{1,0:T(8,128)(2,1)S(1)}, bf16[112,64]{1,0:T(8,128)(2,1)S(1)}, f32[4,272,128]{2,1,0:T(8,128)S(1)}, f32[8,512]{1,0:T(8,128)S(1)}) custom-call(s32[4]{0:T(128)} %sunlit_hbm.1, bf16[7,32,512]{2,1,0:T(8,128)(2,1)} %gases_hbm.1, s32[32,512]{1,0:T(8,128)} %bins_hbm.1, bf16[512]{0:T(512)(128)(2,1)} %cosine_hbm.1, ...), custom_call_target="tpu_custom_call" | custom-call | tf_op jit(solution)/shard_map/pallas_call | solution.py:331
  1.4 7.3 %all-to-all-start = ((s32[8,1,1]{2,1,0:T(1,128)}), s32[8,1,1]{2,1,0:T(1,128)S(1)}, u32[]{:S(2)}, u32[]{:S(2)}) async-start(s32[8,1,1]{2,1,0:T(1,128)} %get-tuple-element.14), calls=%async_computation | async-start | bytes 8192 | tf_op jit(solution)/shard_map/all_to_all | solution.py:368
  8.7 11.0 %shard_map.92.heat_ref = f32[32,512]{1,0:T(8,128)S(1)} custom-call(bf16[32,512]{1,0:T(8,128)(2,1)} %mass_hbm.1, bf16[112,448]{1,0:T(8,128)(2,1)S(1)} %get-tuple-element.10.table_ref, bf16[112,64]{1,0:T(8,128)(2,1)S(1)} %get-tuple-element.11.scatter_ref, f32[4,272,128]{2,1,0:T(8,128)S(1)} %get-tuple-element.12.block_ref), custom_call_target="tpu_custom_call" | custom-call | flops 73400320 | bytes 1048576 | tf_op jit(solution)/shard_map/pallas_call | solution.py:372
  19.7 0.0 all-to-all-done.flags_ref
  19.7 0.7 %shard_map.93 = f32[32,512]{1,0:T(8,128)} custom-call(f32[32,512]{1,0:T(8,128)S(1)} %shard_map.92.heat_ref, f32[8,512]{1,0:T(8,128)S(1)} %get-tuple-element.13.owner_ref, s32[8,1,1]{2,1,0:T(1,128)S(1)} %all-to-all-done.flags_ref), custom_call_target="tpu_custom_call" | custom-call | tf_op jit(solution)/shard_map/pallas_call | solution.py:394
Async XLA Ops:
  1.4 18.3 %all-to-all-start = ((s32[8,1,1]{2,1,0:T(1,128)}), s32[8,1,1]{2,1,0:T(1,128)S(1)}, u32[]{:S(2)}, u32[]{:S(2)}) async-start(s32[8,1,1]{2,1,0:T(1,128)} %get-tuple-element.14), calls=%async_computation | async-start | bytes 8192 | tf_op jit(solution)/shard_map/all_to_all | solution.py:368

commit v2 on v0

--- a/solution.py
+++ b/solution.py
@@ -11,7 +11,7 @@
 LANES = 128
 ROWS = 8
 PACK = 16
-STEP = 8
+STEP = 4
 HALVES = 2
 BIN_ROWS = 64
 LOG2E = math.log2(math.e)
@@ -127,7 +127,8 @@
     heat_ref,
     mass_ref,
     copied,
-    optic_ref,
+    optic_even,
+    optic_odd,
     up_buf,
     rise_buf,
     pass_buf,
@@ -149,7 +150,7 @@
     mass_copy = pltpu.make_async_copy(mass_hbm, mass_ref, copied)
     mass_copy.start()
 
-    def optical(slot, layer):
+    def optical(slot, layer, place_at, optic_ref):
         parts = []
         shape = (BIN_ROWS, LANES)
         rows = lax.broadcasted_iota(jnp.int32, shape, 0).astype(jnp.float32).astype(jnp.bfloat16)
@@ -158,14 +159,14 @@
         selectors = []
         for near in (layer, layer + 1):
             place = bin_row + near
-            bins = jnp.broadcast_to(block_ref[slot, place : place + 1, :], (PACK, LANES)).astype(jnp.bfloat16)
+            bins = jnp.broadcast_to(block_ref[slot, pl.ds(place, 1), :], (PACK, LANES)).astype(jnp.bfloat16)
             bins = jnp.concatenate([bins] * (BIN_ROWS // PACK), axis=0)
             selectors.append(jnp.where(bins == rows, one, zero))
         for gas in range(gas_count):
             pair = []
             for near, selector in zip((layer, layer + 1), selectors):
                 place = gas * levels + near
-                amount = jnp.broadcast_to(block_ref[slot, place : place + 1, :], (PACK, LANES)).astype(jnp.bfloat16)
+                amount = jnp.broadcast_to(block_ref[slot, pl.ds(place, 1), :], (PACK, LANES)).astype(jnp.bfloat16)
                 pair.append(jnp.concatenate([amount] * (BIN_ROWS // PACK), axis=0) * selector)
             parts.append(jnp.concatenate(pair, axis=1))
         weighted = jnp.concatenate(parts, axis=0)
@@ -174,71 +175,69 @@
         albedo = jnp.dot(scatter_ref[...], selected, preferred_element_type=jnp.float32)
         for near in range(2):
             cols = slice(near * LANES, (near + 1) * LANES)
-            optic_ref[layer + near, :points] = tau[:, cols]
-            optic_ref[layer + near, points:] = albedo[:, cols]
-
-    def advance(first, part, cosine, slope):
+            optic_ref[place_at + near, :points] = tau[:, cols]
+            optic_ref[place_at + near, points:] = albedo[:, cols]
+
+    def advance(first, part, slope, optic_ref):
         rows = slice(part * half, (part + 1) * half)
         half_rows = slice(points + part * half, points + (part + 1) * half)
         shape = (vregs, ROWS, LANES)
-        if first > 0:
-            refl = refl_buf[rows].reshape(shape)
-            fall = fall_buf[rows].reshape(shape)
-            direct = direct_buf[rows].reshape(shape)
-        else:
-            direct = jnp.broadcast_to(cosine[None], shape)
-        for layer in range(first, first + STEP):
-            tau = optic_ref[layer, rows].reshape(shape)
-            half_albedo = optic_ref[layer, half_rows].reshape(shape)
+        refl = refl_buf[rows].reshape(shape)
+        fall = fall_buf[rows].reshape(shape)
+        direct = direct_buf[rows].reshape(shape)
+        for slot in range(STEP):
+            layer = first + slot
+            tau = optic_ref[slot, rows].reshape(shape)
+            half_albedo = optic_ref[slot, half_rows].reshape(shape)
             fading = jnp.exp2(tau * (-1.66 * LOG2E))
             passed = jnp.exp2(tau * slope)
             reflect = half_albedo * (1.0 - fading)
             transmit = fading + reflect
             below = direct * passed
             source = half_albedo * (direct - below)
-            if layer == 0:
-                up_buf[layer, rows] = transmit.reshape(half, LANES)
-                rise_buf[layer, rows] = source.reshape(half, LANES)
-                fall = source
-                refl = reflect
-            else:
-                pass_buf[layer, rows] = (1.0 - refl).reshape(half, LANES)
-                inverse = pl.reciprocal(1.0 - reflect * refl, approx=True)
-                up = transmit * inverse
-                rise = (reflect * fall + source) * inverse
-                up_buf[layer, rows] = up.reshape(half, LANES)
-                rise_buf[layer, rows] = rise.reshape(half, LANES)
-                fall = source + transmit * (fall + refl * rise)
-                refl = reflect + transmit * (refl * up)
+            pass_buf[layer, rows] = (1.0 - refl).reshape(half, LANES)
+            inverse = pl.reciprocal(1.0 - reflect * refl, approx=True)
+            up = transmit * inverse
+            rise = (reflect * fall + source) * inverse
+            up_buf[layer, rows] = up.reshape(half, LANES)
+            rise_buf[layer, rows] = rise.reshape(half, LANES)
+            fall = source + transmit * (fall + refl * rise)
+            refl = reflect + transmit * (refl * up)
             direct = below
             gain_buf[part, layer + 1] = jnp.sum(direct + fall, axis=0)
         refl_buf[rows] = refl.reshape(half, LANES)
         fall_buf[rows] = fall.reshape(half, LANES)
         direct_buf[rows] = direct.reshape(half, LANES)
 
-    lead = range(0, STEP, 2)
+    pairs = range(0, STEP, 2)
+    whole = (points // ROWS, ROWS, LANES)
 
     def column_block(block, carry):
         cosine = block_ref[block, ray_row : ray_row + ROWS]
+        albedo = block_ref[block, ray_row + ROWS : ray_row + 2 * ROWS]
         slope = (-LOG2E) / cosine
+        refl_buf[...] = jnp.zeros_like(refl_buf)
+        fall_buf[...] = jnp.zeros_like(fall_buf)
+        direct_buf[...] = jnp.broadcast_to(cosine[:1], direct_buf.shape)
         for part in range(HALVES):
             gain_buf[part, 0] = cosine * float(vregs)
-        for first in range(0, levels, STEP):
-            coming = [layer for layer in range(first + STEP, first + 2 * STEP, 2) if layer < levels]
+
+        def down(turn, inner):
+            first = turn * (2 * STEP)
+            wraps = first + 2 * STEP >= levels
+            next_block = jnp.where(wraps, jnp.minimum(block + 1, blocks - 1), block)
+            next_first = jnp.where(wraps, 0, first + 2 * STEP)
             for part in range(HALVES):
-                for layer in coming[part * len(coming) // HALVES : (part + 1) * len(coming) // HALVES]:
-                    optical(block, layer)
-                advance(first, part, cosine, slope)
-
-        following = jnp.minimum(block + 1, blocks - 1)
-        for layer in lead:
-            optical(following, layer)
-
-        albedo = block_ref[block, ray_row + ROWS : ray_row + 2 * ROWS]
-        shape = (points // ROWS, ROWS, LANES)
-        refl = refl_buf[...].reshape(shape)
-        arriving = (fall_buf[...] + direct_buf[...]).reshape(shape)
-        rising = albedo * arriving * pl.reciprocal(1.0 - albedo * refl, approx=True)
+                for near in pairs[part * len(pairs) // HALVES : (part + 1) * len(pairs) // HALVES]:
+                    optical(block, first + STEP + near, near, optic_odd)
+                advance(first, part, slope, optic_even)
+            for part in range(HALVES):
+                for near in pairs[part * len(pairs) // HALVES : (part + 1) * len(pairs) // HALVES]:
+                    optical(next_block, next_first + near, near, optic_even)
+                advance(first + STEP, part, slope, optic_odd)
+            return inner
+
+        lax.fori_loop(0, levels // (2 * STEP), down, 0)
 
         def total(level):
             summed = gain_buf[0, level]
@@ -246,16 +245,28 @@
                 summed = summed + gain_buf[part, level]
             return summed
 
-        net_buf[levels] = total(levels) - jnp.sum(rising * (1.0 - refl), axis=0)
-        for layer in range(levels - 1, -1, -1):
-            rising = up_buf[layer].reshape(shape) * rising + rise_buf[layer].reshape(shape)
-            taken = rising if layer == 0 else rising * pass_buf[layer].reshape(shape)
-            net_buf[layer] = total(layer) - jnp.sum(taken, axis=0)
+        refl = refl_buf[...].reshape(whole)
+        arriving = (fall_buf[...] + direct_buf[...]).reshape(whole)
+        started = albedo * arriving * pl.reciprocal(1.0 - albedo * refl, approx=True)
+        fall_buf[...] = started.reshape(points, LANES)
+        net_buf[levels] = total(levels) - jnp.sum(started * (1.0 - refl), axis=0)
+
+        def ascend(turn, inner):
+            last = levels - 1 - turn * (2 * STEP)
+            rising = fall_buf[...].reshape(whole)
+            for slot in range(2 * STEP):
+                layer = last - slot
+                rising = up_buf[layer].reshape(whole) * rising + rise_buf[layer].reshape(whole)
+                net_buf[layer] = total(layer) - jnp.sum(rising * pass_buf[layer].reshape(whole), axis=0)
+            fall_buf[...] = rising.reshape(points, LANES)
+            return inner
+
+        lax.fori_loop(0, levels // (2 * STEP), ascend, 0)
         warm_ref[block] = jnp.sum(net_buf[:levels] - net_buf[1:], axis=1)
         return carry
 
-    for layer in lead:
-        optical(0, layer)
+    for near in pairs:
+        optical(0, near, near, optic_even)
     lax.fori_loop(0, blocks, column_block, 0)
     mass_copy.wait()
 
@@ -345,7 +356,8 @@
         scratch_shapes=[
             pltpu.VMEM(layer_mass.shape, layer_mass.dtype),
             pltpu.SemaphoreType.DMA(()),
-            pltpu.VMEM((levels, 2 * points, LANES), jnp.float32),
+            pltpu.VMEM((STEP, 2 * points, LANES), jnp.float32),
+            pltpu.VMEM((STEP, 2 * points, LANES), jnp.float32),
             field,
             field,
             field,

time: 20 us -> 21.6 us (1.080)
  Pallas kernels: 12.5 us -> 14.1 us
    pallas_call x1, Pallas kernels: 10.4 us -> 12 us  [local(): pl.pallas_call(heating_kernel, out_shape=jax.ShapeDtypeStruct((levels, co...]
  transfers between devices with their start and end apart: 1 -> 1, of which waited for: 0 -> 0; matrix products, arithmetic and copies ran while one was open for 0% -> 0% of each run, Pallas kernels for 53% -> 56%
where the time goes in v2:
time: 21.6 us; the launch traced here: 21.4 us
  Pallas kernels  14.1 us (65%)
  starting transfers between devices  7.29 us (34%)
    pallas_call x1, Pallas kernels, local(): pl.pallas_call(heating_kernel, out_shape=jax.ShapeDtypeStruct((levels, co...  12 us
    all_to_all x1, starting transfers between devices, local(): lax.all_to_all(wanted, 'span', split_axis=0, concat_axis=0, tiled=True)  7.29 us
    pallas_call x1, Pallas kernels, local(): pl.pallas_call(functools.partial(prepare_kernel, columns // group_size),...  1.37 us
    pallas_call x1, Pallas kernels, local(): pl.pallas_call(shade_kernel, out_shape=jax.ShapeDtypeStruct((levels, colu...  0.71 us
  transfers between devices with their start and end apart: 1, of which 0 were waited for; matrix products, arithmetic and copies ran while one was open for 0% of the time, Pallas kernels for 56%

profile of v2, /device:TPU:0, one launch (start us, length us, event | category | flops | bytes accessed | tf_op | source)
XLA Modules:
  0.0 21.4 jit_solution(11525458873540036174)
XLA Ops:
  0.0 1.4 %shard_map.91 = (s32[8,1,1]{2,1,0:T(1,128)}, bf16[112,448]{1,0:T(8,128)(2,1)S(1)}, bf16[112,64]{1,0:T(8,128)(2,1)S(1)}, f32[4,272,128]{2,1,0:T(8,128)S(1)}, f32[8,512]{1,0:T(8,128)S(1)}) custom-call(s32[4]{0:T(128)} %sunlit_hbm.1, bf16[7,32,512]{2,1,0:T(8,128)(2,1)} %gases_hbm.1, s32[32,512]{1,0:T(8,128)} %bins_hbm.1, bf16[512]{0:T(512)(128)(2,1)} %cosine_hbm.1, ...), custom_call_target="tpu_custom_call" | custom-call | tf_op jit(solution)/shard_map/pallas_call | solution.py:311
  1.4 7.3 %all-to-all-start = ((s32[8,1,1]{2,1,0:T(1,128)}), s32[8,1,1]{2,1,0:T(1,128)S(1)}, u32[]{:S(2)}, u32[]{:S(2)}) async-start(s32[8,1,1]{2,1,0:T(1,128)} %get-tuple-element.14), calls=%async_computation | async-start | bytes 8192 | tf_op jit(solution)/shard_map/all_to_all | solution.py:348
  8.7 12.0 %shard_map.92.heat_ref = f32[32,512]{1,0:T(8,128)S(1)} custom-call(bf16[32,512]{1,0:T(8,128)(2,1)} %mass_hbm.1, bf16[112,448]{1,0:T(8,128)(2,1)S(1)} %get-tuple-element.10.table_ref, bf16[112,64]{1,0:T(8,128)(2,1)S(1)} %get-tuple-element.11.scatter_ref, f32[4,272,128]{2,1,0:T(8,128)S(1)} %get-tuple-element.12.block_ref), custom_call_target="tpu_custom_call" | custom-call | flops 73400320 | bytes 1048576 | tf_op jit(solution)/shard_map/pallas_call | solution.py:351
  20.7 0.0 all-to-all-done.flags_ref
  20.7 0.7 %shard_map.93 = f32[32,512]{1,0:T(8,128)} custom-call(f32[32,512]{1,0:T(8,128)S(1)} %shard_map.92.heat_ref, f32[8,512]{1,0:T(8,128)S(1)} %get-tuple-element.13.owner_ref, s32[8,1,1]{2,1,0:T(1,128)S(1)} %all-to-all-done.flags_ref), custom_call_target="tpu_custom_call" | custom-call | tf_op jit(solution)/shard_map/pallas_call | solution.py:376
Async XLA Ops:
  1.4 19.3 %all-to-all-start = ((s32[8,1,1]{2,1,0:T(1,128)}), s32[8,1,1]{2,1,0:T(1,128)S(1)}, u32[]{:S(2)}, u32[]{:S(2)}) async-start(s32[8,1,1]{2,1,0:T(1,128)} %get-tuple-element.14), calls=%async_computation | async-start | bytes 8192 | tf_op jit(solution)/shard_map/all_to_all | solution.py:348

commit v3 on v0

--- a/solution.py
+++ b/solution.py
@@ -12,7 +12,7 @@
 ROWS = 8
 PACK = 16
 STEP = 8
-HALVES = 2
+HALVES = 1
 BIN_ROWS = 64
 LOG2E = math.log2(math.e)
 VMEM_BYTES = 24 * 1024 * 1024

time: 20 us -> 20 us (level)
  no operation moved by 1% of the time
where the time goes in v3:
time: 20 us; the launch traced here: 19.8 us
  Pallas kernels  12.5 us (62%)
  starting transfers between devices  7.29 us (36%)
    pallas_call x1, Pallas kernels, local(): pl.pallas_call(heating_kernel, out_shape=jax.ShapeDtypeStruct((levels, co...  10.4 us
    all_to_all x1, starting transfers between devices, local(): lax.all_to_all(wanted, 'span', split_axis=0, concat_axis=0, tiled=True)  7.29 us
    pallas_call x1, Pallas kernels, local(): pl.pallas_call(functools.partial(prepare_kernel, columns // group_size),...  1.37 us
    pallas_call x1, Pallas kernels, local(): pl.pallas_call(shade_kernel, out_shape=jax.ShapeDtypeStruct((levels, colu...  0.71 us
  transfers between devices with their start and end apart: 1, of which 0 were waited for; matrix products, arithmetic and copies ran while one was open for 0% of the time, Pallas kernels for 53%

profile of v3, /device:TPU:0, one launch (start us, length us, event | category | flops | bytes accessed | tf_op | source)
XLA Modules:
  0.0 19.8 jit_solution(10337230872535016126)
XLA Ops:
  0.0 1.4 %shard_map.91 = (s32[8,1,1]{2,1,0:T(1,128)}, bf16[112,448]{1,0:T(8,128)(2,1)S(1)}, bf16[112,64]{1,0:T(8,128)(2,1)S(1)}, f32[4,272,128]{2,1,0:T(8,128)S(1)}, f32[8,512]{1,0:T(8,128)S(1)}) custom-call(s32[4]{0:T(128)} %sunlit_hbm.1, bf16[7,32,512]{2,1,0:T(8,128)(2,1)} %gases_hbm.1, s32[32,512]{1,0:T(8,128)} %bins_hbm.1, bf16[512]{0:T(512)(128)(2,1)} %cosine_hbm.1, ...), custom_call_target="tpu_custom_call" | custom-call | tf_op jit(solution)/shard_map/pallas_call | solution.py:300
  1.4 7.3 %all-to-all-start = ((s32[8,1,1]{2,1,0:T(1,128)}), s32[8,1,1]{2,1,0:T(1,128)S(1)}, u32[]{:S(2)}, u32[]{:S(2)}) async-start(s32[8,1,1]{2,1,0:T(1,128)} %get-tuple-element.14), calls=%async_computation | async-start | bytes 8192 | tf_op jit(solution)/shard_map/all_to_all | solution.py:337
  8.7 10.4 %shard_map.92.heat_ref = f32[32,512]{1,0:T(8,128)S(1)} custom-call(bf16[32,512]{1,0:T(8,128)(2,1)} %mass_hbm.1, bf16[112,448]{1,0:T(8,128)(2,1)S(1)} %get-tuple-element.10.table_ref, bf16[112,64]{1,0:T(8,128)(2,1)S(1)} %get-tuple-element.11.scatter_ref, f32[4,272,128]{2,1,0:T(8,128)S(1)} %get-tuple-element.12.block_ref), custom_call_target="tpu_custom_call" | custom-call | flops 73400320 | bytes 1048576 | tf_op jit(solution)/shard_map/pallas_call | solution.py:340
  19.1 0.0 all-to-all-done.flags_ref
  19.1 0.7 %shard_map.93 = f32[32,512]{1,0:T(8,128)} custom-call(f32[32,512]{1,0:T(8,128)S(1)} %shard_map.92.heat_ref, f32[8,512]{1,0:T(8,128)S(1)} %get-tuple-element.13.owner_ref, s32[8,1,1]{2,1,0:T(1,128)S(1)} %all-to-all-done.flags_ref), custom_call_target="tpu_custom_call" | custom-call | tf_op jit(solution)/shard_map/pallas_call | solution.py:364
Async XLA Ops:
  1.4 17.7 %all-to-all-start = ((s32[8,1,1]{2,1,0:T(1,128)}), s32[8,1,1]{2,1,0:T(1,128)S(1)}, u32[]{:S(2)}, u32[]{:S(2)}) async-start(s32[8,1,1]{2,1,0:T(1,128)} %get-tuple-element.14), calls=%async_computation | async-start | bytes 8192 | tf_op jit(solution)/shard_map/all_to_all | solution.py:337

commit v4 on v0

--- a/solution.py
+++ b/solution.py
@@ -226,9 +226,9 @@
         for first in range(0, levels, STEP):
             coming = [layer for layer in range(first + STEP, first + 2 * STEP, 2) if layer < levels]
             for part in range(HALVES):
+                advance(first, part, cosine, slope)
                 for layer in coming[part * len(coming) // HALVES : (part + 1) * len(coming) // HALVES]:
                     optical(block, layer)
-                advance(first, part, cosine, slope)
 
         following = jnp.minimum(block + 1, blocks - 1)
         for layer in lead:

time: 20 us -> 20 us (level)
  no operation moved by 1% of the time
where the time goes in v4:
time: 20 us; the launch traced here: 19.8 us
  Pallas kernels  12.5 us (62%)
  starting transfers between devices  7.29 us (36%)
    pallas_call x1, Pallas kernels, local(): pl.pallas_call(heating_kernel, out_shape=jax.ShapeDtypeStruct((levels, co...  10.4 us
    all_to_all x1, starting transfers between devices, local(): lax.all_to_all(wanted, 'span', split_axis=0, concat_axis=0, tiled=True)  7.29 us
    pallas_call x1, Pallas kernels, local(): pl.pallas_call(functools.partial(prepare_kernel, columns // group_size),...  1.37 us
    pallas_call x1, Pallas kernels, local(): pl.pallas_call(shade_kernel, out_shape=jax.ShapeDtypeStruct((levels, colu...  0.71 us
  transfers between devices with their start and end apart: 1, of which 0 were waited for; matrix products, arithmetic and copies ran while one was open for 0% of the time, Pallas kernels for 53%

profile of v4, /device:TPU:0, one launch (start us, length us, event | category | flops | bytes accessed | tf_op | source)
XLA Modules:
  0.0 19.8 jit_solution(10652876998256677947)
XLA Ops:
  0.0 1.4 %shard_map.91 = (s32[8,1,1]{2,1,0:T(1,128)}, bf16[112,448]{1,0:T(8,128)(2,1)S(1)}, bf16[112,64]{1,0:T(8,128)(2,1)S(1)}, f32[4,272,128]{2,1,0:T(8,128)S(1)}, f32[8,512]{1,0:T(8,128)S(1)}) custom-call(s32[4]{0:T(128)} %sunlit_hbm.1, bf16[7,32,512]{2,1,0:T(8,128)(2,1)} %gases_hbm.1, s32[32,512]{1,0:T(8,128)} %bins_hbm.1, bf16[512]{0:T(512)(128)(2,1)} %cosine_hbm.1, ...), custom_call_target="tpu_custom_call" | custom-call | tf_op jit(solution)/shard_map/pallas_call | solution.py:300
  1.4 7.3 %all-to-all-start = ((s32[8,1,1]{2,1,0:T(1,128)}), s32[8,1,1]{2,1,0:T(1,128)S(1)}, u32[]{:S(2)}, u32[]{:S(2)}) async-start(s32[8,1,1]{2,1,0:T(1,128)} %get-tuple-element.14), calls=%async_computation | async-start | bytes 8192 | tf_op jit(solution)/shard_map/all_to_all | solution.py:337
  8.7 10.4 %shard_map.92.heat_ref = f32[32,512]{1,0:T(8,128)S(1)} custom-call(bf16[32,512]{1,0:T(8,128)(2,1)} %mass_hbm.1, bf16[112,448]{1,0:T(8,128)(2,1)S(1)} %get-tuple-element.10.table_ref, bf16[112,64]{1,0:T(8,128)(2,1)S(1)} %get-tuple-element.11.scatter_ref, f32[4,272,128]{2,1,0:T(8,128)S(1)} %get-tuple-element.12.block_ref), custom_call_target="tpu_custom_call" | custom-call | flops 73400320 | bytes 1048576 | tf_op jit(solution)/shard_map/pallas_call | solution.py:340
  19.1 0.0 all-to-all-done.flags_ref
  19.1 0.7 %shard_map.93 = f32[32,512]{1,0:T(8,128)} custom-call(f32[32,512]{1,0:T(8,128)S(1)} %shard_map.92.heat_ref, f32[8,512]{1,0:T(8,128)S(1)} %get-tuple-element.13.owner_ref, s32[8,1,1]{2,1,0:T(1,128)S(1)} %all-to-all-done.flags_ref), custom_call_target="tpu_custom_call" | custom-call | tf_op jit(solution)/shard_map/pallas_call | solution.py:364
Async XLA Ops:
  1.4 17.7 %all-to-all-start = ((s32[8,1,1]{2,1,0:T(1,128)}), s32[8,1,1]{2,1,0:T(1,128)S(1)}, u32[]{:S(2)}, u32[]{:S(2)}) async-start(s32[8,1,1]{2,1,0:T(1,128)} %get-tuple-element.14), calls=%async_computation | async-start | bytes 8192 | tf_op jit(solution)/shard_map/all_to_all | solution.py:337

commit v5 on v4

--- a/solution.py
+++ b/solution.py
@@ -11,7 +11,7 @@
 LANES = 128
 ROWS = 8
 PACK = 16
-STEP = 8
+STEP = 4
 HALVES = 2
 BIN_ROWS = 64
 LOG2E = math.log2(math.e)

time: 20 us -> 19.9 us (level)
  transfers between devices with their start and end apart: 1 -> 1, of which waited for: 0 -> 0; matrix products, arithmetic and copies ran while one was open for 0% -> 0% of each run, Pallas kernels for 53% -> 52%
where the time goes in v5:
time: 19.9 us; the launch traced here: 19.7 us
  Pallas kernels  12.4 us (62%)
  starting transfers between devices  7.29 us (37%)
    pallas_call x1, Pallas kernels, local(): pl.pallas_call(heating_kernel, out_shape=jax.ShapeDtypeStruct((levels, co...  10.3 us
    all_to_all x1, starting transfers between devices, local(): lax.all_to_all(wanted, 'span', split_axis=0, concat_axis=0, tiled=True)  7.29 us
    pallas_call x1, Pallas kernels, local(): pl.pallas_call(functools.partial(prepare_kernel, columns // group_size),...  1.37 us
    pallas_call x1, Pallas kernels, local(): pl.pallas_call(shade_kernel, out_shape=jax.ShapeDtypeStruct((levels, colu...  0.71 us
  transfers between devices with their start and end apart: 1, of which 0 were waited for; matrix products, arithmetic and copies ran while one was open for 0% of the time, Pallas kernels for 52%

profile of v5, /device:TPU:0, one launch (start us, length us, event | category | flops | bytes accessed | tf_op | source)
XLA Modules:
  0.0 19.7 jit_solution(842685016314938908)
XLA Ops:
  0.0 1.4 %shard_map.91 = (s32[8,1,1]{2,1,0:T(1,128)}, bf16[112,448]{1,0:T(8,128)(2,1)S(1)}, bf16[112,64]{1,0:T(8,128)(2,1)S(1)}, f32[4,272,128]{2,1,0:T(8,128)S(1)}, f32[8,512]{1,0:T(8,128)S(1)}) custom-call(s32[4]{0:T(128)} %sunlit_hbm.1, bf16[7,32,512]{2,1,0:T(8,128)(2,1)} %gases_hbm.1, s32[32,512]{1,0:T(8,128)} %bins_hbm.1, bf16[512]{0:T(512)(128)(2,1)} %cosine_hbm.1, ...), custom_call_target="tpu_custom_call" | custom-call | tf_op jit(solution)/shard_map/pallas_call | solution.py:300
  1.4 7.3 %all-to-all-start = ((s32[8,1,1]{2,1,0:T(1,128)}), s32[8,1,1]{2,1,0:T(1,128)S(1)}, u32[]{:S(2)}, u32[]{:S(2)}) async-start(s32[8,1,1]{2,1,0:T(1,128)} %get-tuple-element.14), calls=%async_computation | async-start | bytes 8192 | tf_op jit(solution)/shard_map/all_to_all | solution.py:337
  8.7 10.3 %shard_map.92.heat_ref = f32[32,512]{1,0:T(8,128)S(1)} custom-call(bf16[32,512]{1,0:T(8,128)(2,1)} %mass_hbm.1, bf16[112,448]{1,0:T(8,128)(2,1)S(1)} %get-tuple-element.10.table_ref, bf16[112,64]{1,0:T(8,128)(2,1)S(1)} %get-tuple-element.11.scatter_ref, f32[4,272,128]{2,1,0:T(8,128)S(1)} %get-tuple-element.12.block_ref), custom_call_target="tpu_custom_call" | custom-call | flops 73400320 | bytes 1048576 | tf_op jit(solution)/shard_map/pallas_call | solution.py:340
  19.0 0.0 all-to-all-done.flags_ref
  19.0 0.7 %shard_map.93 = f32[32,512]{1,0:T(8,128)} custom-call(f32[32,512]{1,0:T(8,128)S(1)} %shard_map.92.heat_ref, f32[8,512]{1,0:T(8,128)S(1)} %get-tuple-element.13.owner_ref, s32[8,1,1]{2,1,0:T(1,128)S(1)} %all-to-all-done.flags_ref), custom_call_target="tpu_custom_call" | custom-call | tf_op jit(solution)/shard_map/pallas_call | solution.py:364
Async XLA Ops:
  1.4 17.6 %all-to-all-start = ((s32[8,1,1]{2,1,0:T(1,128)}), s32[8,1,1]{2,1,0:T(1,128)S(1)}, u32[]{:S(2)}, u32[]{:S(2)}) async-start(s32[8,1,1]{2,1,0:T(1,128)} %get-tuple-element.14), calls=%async_computation | async-start | bytes 8192 | tf_op jit(solution)/shard_map/all_to_all | solution.py:337

commit v6 on v4

--- a/solution.py
+++ b/solution.py
@@ -12,7 +12,7 @@
 ROWS = 8
 PACK = 16
 STEP = 8
-HALVES = 2
+HALVES = 1
 BIN_ROWS = 64
 LOG2E = math.log2(math.e)
 VMEM_BYTES = 24 * 1024 * 1024

time: 20 us -> 20 us (level)
  no operation moved by 1% of the time
where the time goes in v6:
time: 20 us; the launch traced here: 19.8 us
  Pallas kernels  12.5 us (62%)
  starting transfers between devices  7.29 us (36%)
    pallas_call x1, Pallas kernels, local(): pl.pallas_call(heating_kernel, out_shape=jax.ShapeDtypeStruct((levels, co...  10.4 us
    all_to_all x1, starting transfers between devices, local(): lax.all_to_all(wanted, 'span', split_axis=0, concat_axis=0, tiled=True)  7.29 us
    pallas_call x1, Pallas kernels, local(): pl.pallas_call(functools.partial(prepare_kernel, columns // group_size),...  1.37 us
    pallas_call x1, Pallas kernels, local(): pl.pallas_call(shade_kernel, out_shape=jax.ShapeDtypeStruct((levels, colu...  0.71 us
  transfers between devices with their start and end apart: 1, of which 0 were waited for; matrix products, arithmetic and copies ran while one was open for 0% of the time, Pallas kernels for 53%

profile of v6, /device:TPU:0, one launch (start us, length us, event | category | flops | bytes accessed | tf_op | source)
XLA Modules:
  0.0 19.8 jit_solution(10337230872535016126)
XLA Ops:
  0.0 1.4 %shard_map.91 = (s32[8,1,1]{2,1,0:T(1,128)}, bf16[112,448]{1,0:T(8,128)(2,1)S(1)}, bf16[112,64]{1,0:T(8,128)(2,1)S(1)}, f32[4,272,128]{2,1,0:T(8,128)S(1)}, f32[8,512]{1,0:T(8,128)S(1)}) custom-call(s32[4]{0:T(128)} %sunlit_hbm.1, bf16[7,32,512]{2,1,0:T(8,128)(2,1)} %gases_hbm.1, s32[32,512]{1,0:T(8,128)} %bins_hbm.1, bf16[512]{0:T(512)(128)(2,1)} %cosine_hbm.1, ...), custom_call_target="tpu_custom_call" | custom-call | tf_op jit(solution)/shard_map/pallas_call | solution.py:300
  1.4 7.3 %all-to-all-start = ((s32[8,1,1]{2,1,0:T(1,128)}), s32[8,1,1]{2,1,0:T(1,128)S(1)}, u32[]{:S(2)}, u32[]{:S(2)}) async-start(s32[8,1,1]{2,1,0:T(1,128)} %get-tuple-element.14), calls=%async_computation | async-start | bytes 8192 | tf_op jit(solution)/shard_map/all_to_all | solution.py:337
  8.7 10.4 %shard_map.92.heat_ref = f32[32,512]{1,0:T(8,128)S(1)} custom-call(bf16[32,512]{1,0:T(8,128)(2,1)} %mass_hbm.1, bf16[112,448]{1,0:T(8,128)(2,1)S(1)} %get-tuple-element.10.table_ref, bf16[112,64]{1,0:T(8,128)(2,1)S(1)} %get-tuple-element.11.scatter_ref, f32[4,272,128]{2,1,0:T(8,128)S(1)} %get-tuple-element.12.block_ref), custom_call_target="tpu_custom_call" | custom-call | flops 73400320 | bytes 1048576 | tf_op jit(solution)/shard_map/pallas_call | solution.py:340
  19.1 0.0 all-to-all-done.flags_ref
  19.1 0.7 %shard_map.93 = f32[32,512]{1,0:T(8,128)} custom-call(f32[32,512]{1,0:T(8,128)S(1)} %shard_map.92.heat_ref, f32[8,512]{1,0:T(8,128)S(1)} %get-tuple-element.13.owner_ref, s32[8,1,1]{2,1,0:T(1,128)S(1)} %all-to-all-done.flags_ref), custom_call_target="tpu_custom_call" | custom-call | tf_op jit(solution)/shard_map/pallas_call | solution.py:364
Async XLA Ops:
  1.4 17.7 %all-to-all-start = ((s32[8,1,1]{2,1,0:T(1,128)}), s32[8,1,1]{2,1,0:T(1,128)S(1)}, u32[]{:S(2)}, u32[]{:S(2)}) async-start(s32[8,1,1]{2,1,0:T(1,128)} %get-tuple-element.14), calls=%async_computation | async-start | bytes 8192 | tf_op jit(solution)/shard_map/all_to_all | solution.py:337
